TPU v7x, 512 devices: a whole 4x8x8 slice. The times are simulated.
512 devices in a mesh: page: 16 (over z, core), row: 32 (over x, y).
Axes of the slice: x: 4, y: 8, z: 8, core: 2. Of those that a mesh axis runs over, the one named last changes fastest.
Arguments:
- qkv_rows: bfloat16 [16, 2048, 3840], P('page', 'row'), may hold values from -12 to 12
- residual: bfloat16 [16, 2048, 1280], P('page', 'row'), may hold values from -40 to 40
- out_weight: bfloat16 [1280, 1280], P('page'), may hold values from -0.15625 to 0.15625
- norm_gain: float32 [1280], replicated, may hold values from 0.1 to 1.9
- merge_weight: bfloat16 [5120, 5120], P('row'), may hold values from -0.078125 to 0.078125
- merge_bias: float32 [5120], P('row'), may hold values from -3 to 3
- page_grid: int32 [16, 2], P('page'), may hold values from 2 to 256, as said below
Outputs:
- merged: bfloat16 [16, 5120, 512], P('page', 'row')
Inputs may be any that keep to these rules, and one draw needn't show every extreme that they name: `page_grid`: rows and columns are even; rows times columns is at most 2048, and one page of every draw has exactly 2048 live patches in 256 rows of 8 columns; columns are at least 8.
All inputs are finite; a program needn't handle non-finite values.
Results may differ from a plain program's by a relative error of at most 0.0049.
Values may be sent and summed in bfloat16 or wider, within the bound.
A program may use at most 64 MiB of HBM per device.

v0:
```python
import math

import jax
import jax.numpy as jnp
from jax import lax
from jax.sharding import PartitionSpec as P

D = 1280
HEADS = 16
HDIM = 80


def local(qkv_rows, residual, out_weight, norm_gain, merge_weight, merge_bias, page_grid):
    row_count = lax.axis_size("row")
    q_split = max(1, row_count // HEADS)
    head_groups = row_count // q_split
    width = D // head_groups
    heads_per = width // HDIM
    band_len = qkv_rows.shape[1]
    part_len = band_len // q_split
    local_qkv = qkv_rows[0]
    queries = local_qkv[:, :D]
    key_vals = jnp.concatenate(
        [
            local_qkv[:, D : 2 * D].reshape(band_len, head_groups, width),
            local_qkv[:, 2 * D :].reshape(band_len, head_groups, width),
        ],
        axis=2,
    )
    q_send = (
        queries.reshape(q_split, part_len, head_groups, width)
        .transpose(2, 0, 1, 3)
        .reshape(row_count, part_len, width)
    )
    kv_send = jnp.broadcast_to(
        key_vals.transpose(1, 0, 2)[:, None], (head_groups, q_split, band_len, 2 * width)
    )
    kv_send = kv_send.reshape(row_count, band_len, 2 * width)
    q_recv, kv_recv = (
        lax.all_to_all(q_send, "row", split_axis=0, concat_axis=1, tiled=True),
        lax.all_to_all(kv_send, "row", split_axis=0, concat_axis=1, tiled=True),
    )
    kv_local = kv_recv[0]
    positions = jnp.arange(row_count * band_len, dtype=jnp.int32)
    valid_len = page_grid[0, 0] * page_grid[0, 1]
    key_valid = positions < valid_len
    key_total = kv_local.shape[0]
    key_heads = kv_local[:, :width].reshape(key_total, heads_per, HDIM)
    value_heads = kv_local[:, width:].reshape(key_total, heads_per, HDIM)
    query_total = row_count * part_len
    q_block = math.gcd(query_total, 512)
    q_blocks = q_recv[0].reshape(query_total // q_block, q_block, heads_per, HDIM)
    root_dim = math.sqrt(HDIM)

    def attend(q_span):
        scores = (
            jnp.einsum("qhd,khd->hqk", q_span, key_heads, preferred_element_type=jnp.float32)
            / root_dim
        )
        scores = jnp.where(key_valid[None, None, :], scores, -1e30)
        peak = jnp.max(scores, axis=2, keepdims=True)
        weights = jnp.exp(scores - peak)
        total = jnp.sum(weights, axis=2, keepdims=True)
        mixed = (
            jnp.einsum(
                "hqk,khd->hqd",
                weights.astype(jnp.bfloat16),
                value_heads,
                preferred_element_type=jnp.float32,
            )
            / total
        )
        return mixed.transpose(1, 0, 2).reshape(q_span.shape[0], width).astype(jnp.bfloat16)

    attn_heads = lax.map(attend, q_blocks).reshape(row_count, part_len, width)
    returned = lax.all_to_all(attn_heads, "row", split_axis=0, concat_axis=0, tiled=True)
    attn = (
        returned.reshape(head_groups, q_split, part_len, width)
        .transpose(1, 2, 0, 3)
        .reshape(band_len, D)
    )
    projected = jnp.dot(
        attn,
        lax.all_gather(out_weight, "page", axis=0, tiled=True),
        preferred_element_type=jnp.float32,
    )
    hidden = residual[0].astype(jnp.float32) + projected
    normed = (
        hidden * lax.rsqrt(jnp.mean(hidden * hidden, axis=1, keepdims=True) + 1e-06) * norm_gain
    ).astype(jnp.bfloat16)
    rows_n = page_grid[0, 0]
    cols_n = page_grid[0, 1]
    group_total = band_len * row_count // 4
    slots = jnp.arange(group_total, dtype=jnp.int32)
    half_cols = cols_n // 2
    live = slots < rows_n // 2 * half_cols
    first = jnp.where(live, 2 * (slots // half_cols) * cols_n + 2 * (slots % half_cols), 0)
    corners = [first, first + 1, first + cols_n, first + cols_n + 1]
    local_units = merge_weight.shape[0]
    page_all = lax.all_gather(normed, "row", axis=0, tiled=True)
    merged_sum = jnp.zeros((local_units, group_total), jnp.float32)
    for corner in range(4):
        picked = jnp.take(page_all, corners[corner], axis=0)
        merged_sum = merged_sum + jnp.einsum(
            "md,gd->mg",
            merge_weight[:, corner * D : (corner + 1) * D],
            picked,
            preferred_element_type=jnp.float32,
        )
    merged = jax.nn.gelu(merged_sum + merge_bias[:, None], approximate=False)
    merged = jnp.where(live[None, :], merged, 0.0).astype(jnp.bfloat16)
    return merged[None]


def solution(mesh):
    in_specs = (
        P("page", "row", None),
        P("page", "row", None),
        P("page", None),
        P(),
        P("row", None),
        P("row"),
        P("page", None),
    )
    out_specs = P("page", "row", None)
    return jax.shard_map(local, mesh=mesh, in_specs=in_specs, out_specs=out_specs, check_vma=False)
```

profile of v0, /device:TPU:8, one launch (start us, length us, event | category | flops | bytes accessed | tf_op | source)
XLA Modules:
  0.0 219.9 jit_solution(7898743524473938593)
XLA Ops:
  6.5 0.7 all-gather.3.cloned.1.call-update
  7.3 1.1 fusion.101
  8.4 0.4 reshape.94
  8.8 0.8 copy.20
  9.5 10.2 %all-to-all-start = ((bf16[32,32,80]{2,1,0:T(8,128)(2,1)}), bf16[32,32,80]{2,1,0:T(8,128)(2,1)S(1)}, u32[]{:S(2)}, u32[]{:S(2)}) async-start(bf16[32,32,80]{2,1,0:T(8,128)(2,1)} %bitcast.5), calls=%async_computation | async-start | bytes 524288 | tf_op jit(solution)/shard_map/all_to_all | solution.py:40
  19.7 0.4 reshape.97
  20.1 0.4 reshape.96
  20.5 0.2 maximum_bitcast_fusion
  20.7 0.2 copy.21
  20.9 0.0 copy-start.2
  20.9 11.1 %all-to-all-done = bf16[32,32,80]{2,1,0:T(8,128)(2,1)S(1)} async-done(((bf16[32,32,80]{2,1,0:T(8,128)(2,1)}), bf16[32,32,80]{2,1,0:T(8,128)(2,1)S(1)}, u32[]{:S(2)}, u32[]{:S(2)}) %all-to-all-start) | async-done | bytes 163872 | tf_op jit(solution)/shard_map/all_to_all | solution.py:40
  32.0 1.1 broadcast_in_dim.56
  33.1 4.6 %all-to-all-start.1 = ((bf16[32,64,160]{2,1,0:T(8,128)(2,1)}), bf16[32,64,160]{2,1,0:T(8,128)(2,1)S(1)}, u32[]{:S(2)}, u32[]{:S(2)}) async-start(bf16[32,64,160]{2,1,0:T(8,128)(2,1)} %bitcast.8), calls=%async_computation.1 | async-start | bytes 2097152 | tf_op jit(solution)/shard_map/all_to_all | solution.py:41
  37.7 0.0 all-gather.5.cloned.1.call-start
  37.7 0.6 fusion.102
  39.5 0.1 copy.23
  39.7 25.7 %all-to-all-done.1 = bf16[32,64,160]{2,1,0:T(8,128)(2,1)S(1)} async-done(((bf16[32,64,160]{2,1,0:T(8,128)(2,1)}), bf16[32,64,160]{2,1,0:T(8,128)(2,1)S(1)}, u32[]{:S(2)}, u32[]{:S(2)}) %all-to-all-start.1) | async-done | bytes 655392 | tf_op jit(solution)/shard_map/all_to_all | solution.py:41
  65.4 0.3 fusion.100
  65.6 0.2 copy.27
  65.8 0.2 copy.28
  66.0 5.9 %while.11 = (s32[]{:T(128)}, bf16[2,512,80]{1,2,0:T(8,128)(2,1)S(1)}, bf16[2,512,1,80]{1,3,2,0:T(8,128)(2,1)S(1)}, bf16[2048,1,80]{0,2,1:T(8,128)(2,1)S(1)}, bf1...) while((s32[]{:T(128)}, bf16[2,512,80]{1,2,0:T(8,128)(2,1)S(1)}, ...), condition=%wide.region_3.4_spmd.clone, body=%wide.region_0.3_spmd.clone.sunk | while | flops 347161600 | bytes 13420641 | solution.py:75
  66.1 0.9 fusion.112
  67.0 0.9 fusion.113
  67.9 1.1 fusion.114
  69.0 0.9 fusion.112
  69.9 0.9 fusion.113
  70.9 1.1 fusion.114
  71.9 0.0 copy-start
  71.9 0.2 copy.24
  72.1 16.5 %all_to_all.23 = bf16[32,32,80]{2,1,0:T(8,128)(2,1)S(1)} all-to-all(bf16[32,32,80]{2,1,0:T(8,128)(2,1)S(1)} %bitcast.123), channel_id=1, replica_groups=mesh['page'=16,'row'=32] {'row'}, dimensions={0} | all-to-all | bytes 327680 | tf_op jit(solution)/shard_map/all_to_all | solution.py:76
  88.6 0.2 copy.30
  88.8 0.3 reshape.103
  89.1 0.0 all-gather.3.cloned.1.call-done
  89.1 2.7 %multiply_reduce_fusion = (f32[64]{0:T(128)S(1)}, f32[64,1280]{1,0:T(8,128)S(1)}) fusion(bf16[64,1280]{1,0:T(8,128)(2,1)S(1)} %reshape.103, bf16[1280,1280]{1,0:T(8,128)(2,1)} %all-gather.3.cloned.1.call-done, bf16[1,64,1280]{2,1,0:T(8,128)(2,1)S(1)} %copy-done), kind=kOutput, calls=%fused_computation.78 | convolution fusion | flops 210042816 | bytes 3932416 | tf_op jit(solution)/shard_map/dot_general | solution.py:82
  91.9 0.8 multiply_convert_fusion
  92.7 0.0 all-gather.5.cloned.1.call-update
  98.1 0.1 compare_select_fusion.3
  98.2 0.1 compare_and_fusion.2
  98.4 0.8 compare_and_fusion
  99.2 83.0 %all-gather.5.cloned.1.call-done = bf16[2048,1280]{1,0:T(8,128)(2,1)} async-done(((bf16[64,1280]{1,0:T(8,128)(2,1)}), bf16[2048,1280]{1,0:T(8,128)(2,1)}) %all-gather.5.cloned.1.call-update) | async-done | bytes 5242896 | tf_op jit(solution)/shard_map/all_gather | solution.py:100
  182.2 6.3 %gather_fusion.1 = bf16[512,1280]{1,0:T(8,128)(2,1)S(1)} fusion(bf16[2048,1280]{1,0:T(8,128)(2,1)} %all-gather.5.cloned.1.call-done, s32[1024]{0:T(1024)S(1)} %pad_clamp_fusion.2), kind=kCustom, calls=%fused_computation.1.clone | custom fusion | bytes 2623488 | tf_op jit(solution)/shard_map/jit(_take)/gather | solution.py:103
  188.5 0.7 fusion.32
  189.1 6.3 %gather_fusion = bf16[512,1280]{1,0:T(8,128)(2,1)S(1)} fusion(bf16[2048,1280]{1,0:T(8,128)(2,1)} %all-gather.5.cloned.1.call-done, s32[1024]{0:T(1024)S(1)} %pad_clamp_fusion.3), kind=kCustom, calls=%fused_computation.clone | custom fusion | bytes 2623488 | tf_op jit(solution)/shard_map/jit(_take)/gather | solution.py:103
  195.4 1.4 fusion.40
  196.8 6.3 %gather_fusion.2 = bf16[512,1280]{1,0:T(8,128)(2,1)S(1)} fusion(bf16[2048,1280]{1,0:T(8,128)(2,1)} %all-gather.5.cloned.1.call-done, s32[1024]{0:T(1024)S(1)} %pad_clamp_fusion.1), kind=kCustom, calls=%fused_computation.2.clone | custom fusion | bytes 2623488 | tf_op jit(solution)/shard_map/jit(_take)/gather | solution.py:103
  203.1 1.6 fusion.43
  204.8 6.3 %gather_fusion.3 = bf16[512,1280]{1,0:T(8,128)(2,1)S(1)} fusion(bf16[2048,1280]{1,0:T(8,128)(2,1)} %all-gather.5.cloned.1.call-done, s32[1024]{0:T(1024)S(1)} %pad_clamp_fusion), kind=kCustom, calls=%fused_computation.3.clone | custom fusion | bytes 2623488 | tf_op jit(solution)/shard_map/jit(_take)/gather | solution.py:103
  211.1 2.0 fusion.83
  (18 shorter events, 0.1 us)
Async XLA Ops:
  6.5 82.6 %all-gather.3.cloned.1.call-start = ((), (), s32[]{:S(2)}) async-start(), calls=%async_computation.3 | async-start | bytes 3481600 | tf_op jit(solution)/shard_map/all_gather | solution.py:84
  9.5 22.5 %all-to-all-start = ((bf16[32,32,80]{2,1,0:T(8,128)(2,1)}), bf16[32,32,80]{2,1,0:T(8,128)(2,1)S(1)}, u32[]{:S(2)}, u32[]{:S(2)}) async-start(bf16[32,32,80]{2,1,0:T(8,128)(2,1)} %bitcast.5), calls=%async_computation | async-start | bytes 524288 | tf_op jit(solution)/shard_map/all_to_all | solution.py:40
  20.9 16.8 %copy-start.2 = (s32[1,2]{1,0:T(1,128)S(1)}, s32[1,2]{1,0:T(1,128)}, u32[]{:S(2)}) copy-start(s32[1,2]{1,0:T(1,128)} %param.17) | copy-start | bytes 28
  33.1 32.3 %all-to-all-start.1 = ((bf16[32,64,160]{2,1,0:T(8,128)(2,1)}), bf16[32,64,160]{2,1,0:T(8,128)(2,1)S(1)}, u32[]{:S(2)}, u32[]{:S(2)}) async-start(bf16[32,64,160]{2,1,0:T(8,128)(2,1)} %bitcast.8), calls=%async_computation.1 | async-start | bytes 2097152 | tf_op jit(solution)/shard_map/all_to_all | solution.py:41
  37.7 144.5 %all-gather.5.cloned.1.call-start = ((), (), s32[]{:S(2)}) async-start(), calls=%async_computation.4 | async-start | bytes 5406720 | tf_op jit(solution)/shard_map/all_gather | solution.py:100
  71.9 17.2 %copy-start = (bf16[1,64,1280]{2,1,0:T(8,128)(2,1)S(1)}, bf16[1,64,1280]{2,1,0:T(8,128)(2,1)}, u32[]{:S(2)}) copy-start(bf16[1,64,1280]{2,1,0:T(8,128)(2,1)} %param.12) | copy-start | bytes 491524
  89.1 2.8 %copy-start.1 = (f32[1280]{0:T(1024)S(1)}, f32[1280]{0:T(1024)}, u32[]{:S(2)}) copy-start(f32[1280]{0:T(1024)} %param.14) | copy-start | bytes 15364
  99.2 89.3 %copy-start.3 = (bf16[160,5120]{1,0:T(8,128)(2,1)S(1)}, bf16[160,5120]{1,0:T(8,128)(2,1)}, u32[]{:S(2)}) copy-start(bf16[160,5120]{1,0:T(8,128)(2,1)} %param.15) | copy-start | bytes 4915204
  204.8 6.3 %copy-start.4 = (f32[160]{0:T(256)S(1)}, f32[160]{0:T(256)}, u32[]{:S(2)}) copy-start(f32[160]{0:T(256)} %param.16) | copy-start | bytes 1924
Sparse Core Ops, SparseCore 0:
  9.5 49.1 all-gather.2
  92.8 89.3 all-gather.4
where the time goes:
time: 221 us; the launch traced here: 220 us
  waiting for transfers between devices  121 us (55%)
  local copies, waits for them, and re-layouts  31.4 us (14%)
  between operations  20.3 us (9%)
  blocking collectives  16.5 us (7%)
  starting transfers between devices  14.8 us (7%)
  matrix products  12.4 us (6%)
  other arithmetic  3.99 us (2%)
    all_gather x1, waiting for transfers between devices, local(): page_all = lax.all_gather(normed, 'row', axis=0, tiled=True)  83 us
    all_to_all x1, waiting for transfers between devices, local(): lax.all_to_all(kv_send, 'row', split_axis=0, concat_axis=1, tiled=True)  25.7 us
    gather x4, local copies, waits for them, and re-layouts, local(): picked = jnp.take(page_all, corners[corner], axis=0)  25.1 us
    all_to_all x1, blocking collectives, local(): lax.all_to_all(attn_heads, 'row', split_axis=0, concat_axis=0, tiled=True)  16.5 us
    all_to_all x1, waiting for transfers between devices, local(): lax.all_to_all(q_send, 'row', split_axis=0, concat_axis=1, tiled=True)  11.1 us
    all_to_all x1, starting transfers between devices, local(): lax.all_to_all(q_send, 'row', split_axis=0, concat_axis=1, tiled=True)  10.2 us
    dot_general x4, matrix products, local(): jnp.einsum('md,gd->mg', merge_weight[:, corner * D:(corner + 1) * D], pic...  5.72 us
    all_to_all x1, starting transfers between devices, local(): lax.all_to_all(kv_send, 'row', split_axis=0, concat_axis=1, tiled=True)  4.56 us
  transfers between devices with their start and end apart: 4, of which 3 were waited for; matrix products, arithmetic and copies ran while one was open for 6% of the time, Pallas kernels for 0%

commit v1 on v0

v1 whole, which is shorter than its diff:
```python
import functools
import math

import jax
import jax.numpy as jnp
from jax import lax
from jax.experimental import pallas as pl
from jax.experimental.pallas import tpu as pltpu
from jax.sharding import PartitionSpec as P

D = 1280
HEADS = 16
HDIM = 80
MESH = pl.DeviceIdType.MESH
F32 = jnp.float32
BF16 = jnp.bfloat16
BIG = -1e30


def rcopy(src, dst, send_sem, recv_sem, dev):
    return pltpu.make_async_remote_copy(
        src_ref=src, dst_ref=dst, send_sem=send_sem, recv_sem=recv_sem,
        device_id=dev, device_id_type=MESH,
    )


def nt(a, b):
    return lax.dot_general(a, b, (((1,), (1,)), ((), ())), preferred_element_type=F32)


def kernel(
    grid_ref, qkv_ref, res_ref, wo_ref, gain_ref, bias_ref, w_ref,
    out_ref,
    pack_buf, xbuf, obuf, abuf, wo_pad, wsl, nsend, nall, own_part, part_send, part_recv,
    p1_send, p1_recv, fw_send, fw_recv, ret_send, ret_recv,
    w_send, w_recv, wf_send, wf_recv,
    z_send, z_recv, zf_send, zf_recv,
    xa_send, xa_recv, y_send, y_recv, rs_send, rs_recv, loc_sem,
):
    page = lax.axis_index("page")
    row = lax.axis_index("row")
    core = page % 2
    zi = page // 2
    par = row % 2
    me16 = row // 2
    xi = row // 8
    yi = row % 8
    peer_page = page - core + par
    sib = (page - core + 1 - core, row)
    is_self = par == core
    y_right = (page, xi * 8 + (yi + 1) % 8)
    y_left = (page, xi * 8 + (yi + 7) % 8)
    z_right = (((zi + 1) % 8) * 2 + core, row)
    z_left = (((zi + 7) % 8) * 2 + core, row)

    def xdev(j):
        return (page, ((xi + j) % 4) * 8 + yi)

    def peer(s):
        return (peer_page, 2 * s + core)

    barrier = pltpu.get_barrier_semaphore()

    def greet(dev):
        pl.semaphore_signal(barrier, inc=1, device_id=dev, device_id_type=MESH)

    for dev in (sib, y_right, y_left, z_right, z_left):
        greet(dev)

    def greet_peer(i, carry):
        greet(peer((me16 + i) % 16))
        return carry

    lax.fori_loop(1, 16, greet_peer, 0)

    @pl.when(jnp.logical_not(is_self))
    def _():
        greet(peer(me16))
        for j in (1, 2, 3):
            greet(xdev(j))

    rows_n = grid_ref[0, 0]
    cols_n = grid_ref[0, 1]
    valid_len = rows_n * cols_n
    lane = lax.broadcasted_iota(jnp.int32, (64, 256), 1)
    slot = row * 64 + lax.broadcasted_iota(jnp.int32, (64, 256), 0)
    tail = jnp.where(
        lane == 240, jnp.where(slot < valid_len, 0.0, BIG), jnp.where(lane == 241, 1.0, 0.0)
    )
    for h in range(HEADS):
        val = tail
        for third in (2, 1, 0):
            start = third * D + h * HDIM
            base = min(start // 128 * 128, 3 * D - 256)
            dest = third * HDIM
            window = qkv_ref[0, :, base : base + 256].astype(F32)
            shift = (dest - (start - base)) % 256
            if shift:
                window = pltpu.roll(window, shift, axis=1)
            val = jnp.where((lane >= dest) & (lane < dest + HDIM), window, val)
        pack_buf[h] = val.astype(BF16)

    @pl.when(is_self)
    def _():
        pl.semaphore_wait(barrier, 20)

    @pl.when(jnp.logical_not(is_self))
    def _():
        pl.semaphore_wait(barrier, 24)

    def z_slot(ref, dist, direction, half):
        src_z = (zi - dist + 8) % 8 if direction == 0 else (zi + dist) % 8
        return ref.at[src_z * 2 + core, 32:112, half * 640 : half * 640 + 640]

    def z_limit(direction, half):
        return 4 if direction == half else 3

    def z_copy(dist, direction, half):
        if dist == 1:
            src = wo_ref.at[:, half * 640 : half * 640 + 640]
        else:
            src = z_slot(wo_pad, dist - 1, direction, half)
        return rcopy(
            src, z_slot(wo_pad, dist - 1, direction, half),
            z_send.at[direction, half, dist - 1], z_recv.at[direction, half, dist - 1],
            z_right if direction == 0 else z_left,
        )

    def z_fwd(dist, direction, half):
        place = z_slot(wo_pad, dist, direction, half)
        return rcopy(
            place, place, zf_send.at[direction, half, dist - 1],
            zf_recv.at[direction, half, dist - 1], sib,
        )

    for direction in (0, 1):
        for half in (0, 1):
            z_copy(1, direction, half).start()

    def p1_copy(i):
        h = (me16 + i) % 16
        return rcopy(
            pack_buf.at[h], xbuf.at[0, me16], p1_send.at[h], p1_recv.at[me16], peer(h)
        )

    p1_local = pltpu.make_async_copy(pack_buf.at[me16], xbuf.at[0, me16], p1_recv.at[me16])

    @pl.when(is_self)
    def _():
        p1_local.start()

    @pl.when(jnp.logical_not(is_self))
    def _():
        p1_copy(0).start()

    def p1_start(i, carry):
        p1_copy(i).start()
        return carry

    lax.fori_loop(1, 16, p1_start, 0)

    own_wo = pltpu.make_async_copy(wo_ref, wo_pad.at[page, 32:112, :], loc_sem.at[0])
    own_wo.start()
    sib_wo = rcopy(wo_ref, wo_pad.at[page, 32:112, :], loc_sem.at[1], loc_sem.at[2], sib)
    sib_wo.start()
    for h in range(HEADS):
        wo_pad[h, 0:32, :] = jnp.zeros((32, D), BF16)
        wo_pad[h, 112:128, :] = jnp.zeros((16, D), BF16)

    def fw_copy(s):
        return rcopy(xbuf.at[0, s], xbuf.at[1, s], fw_send.at[s], fw_recv.at[s], sib)

    def p1_take(i, carry):
        s = (me16 + 16 - i) % 16
        rcopy(xbuf.at[0, s], xbuf.at[0, s], p1_send.at[s], p1_recv.at[s], sib).wait_recv()
        fw_copy(s).start()
        return carry

    @pl.when(is_self)
    def _():
        p1_local.wait()
        fw_copy(me16).start()

    @pl.when(jnp.logical_not(is_self))
    def _():
        p1_take(0, 0)

    for dist in (1, 2, 3, 4):
        lax.fori_loop(4 * dist - 3, min(16, 4 * dist + 1), p1_take, 0)
        for direction in (0, 1):
            for half in (0, 1):
                if dist > z_limit(direction, half):
                    continue
                place = z_slot(wo_pad, dist, direction, half)
                rcopy(
                    place, place, z_send.at[direction, half, dist - 1],
                    z_recv.at[direction, half, dist - 1], sib,
                ).wait_recv()
                if dist < z_limit(direction, half):
                    z_copy(dist + 1, direction, half).start()
                z_fwd(dist, direction, half).start()

    def w_copy(j, di):
        xd = (xi + j) % 4
        col = pl.multiple_of((2 * di + xd // 2) * D + (xd % 2) * 640, 128)
        lines = pl.ds(pl.multiple_of(core * 80, 16), 80)
        return rcopy(
            w_ref.at[lines, pl.ds(col, 640)], wsl.at[xi, di, lines, :],
            w_send.at[j - 1, di], w_recv.at[j - 1, di], xdev(j),
        )

    def w_fwd(j, di):
        xs = (xi + 4 - j) % 4
        lines = pl.ds(pl.multiple_of(core * 80, 16), 80)
        place = wsl.at[xs, di, lines, :]
        return rcopy(place, place, wf_send.at[j - 1, di], wf_recv.at[j - 1, di], sib)

    for j in (1, 3, 2):
        for di in (0, 1):
            w_copy(j, di).start()
    w_local = []
    for di in (0, 1):
        col = pl.multiple_of((2 * di + xi // 2) * D + (xi % 2) * 640, 128)
        w_local.append(
            pltpu.make_async_copy(w_ref.at[:, pl.ds(col, 640)], wsl.at[xi, di], loc_sem.at[4 + di])
        )
        w_local[di].start()

    def fw_take(s, carry):
        rcopy(xbuf.at[1, s], xbuf.at[1, s], fw_send.at[s], fw_recv.at[s], sib).wait_recv()
        return carry

    lax.fori_loop(0, 16, fw_take, 0)
    factor = math.log2(math.e) / math.sqrt(HDIM)
    lane_q = lax.broadcasted_iota(jnp.int32, (256, 256), 1)

    def ret_copy(s):
        return rcopy(obuf.at[s], abuf.at[me16], ret_send.at[s], ret_recv.at[me16], peer(s))

    ret_local = pltpu.make_async_copy(obuf.at[me16], abuf.at[me16], ret_recv.at[me16])

    def attend(i, carry):
        blk = (i + me16) % 4
        queries = xbuf[0, pl.ds(4 * blk, 4)].reshape(256, 256).astype(F32)
        rolled = pltpu.roll(queries, HDIM, axis=1)
        rolled = jnp.where(
            (lane_q >= HDIM) & (lane_q < 2 * HDIM), rolled, jnp.where(lane_q == 240, 1.0, 0.0)
        ).astype(BF16)
        keys = xbuf[...].reshape(2048, 256)
        scores = nt(rolled, keys)
        peak = jnp.max(scores, axis=1, keepdims=True)
        weights = jnp.exp2((scores - peak) * factor).astype(BF16)
        mixed = jnp.dot(weights, keys, preferred_element_type=F32)[:, 128:]
        mixed = mixed / mixed[:, 113:114]
        obuf[pl.ds(4 * blk, 4)] = mixed.astype(BF16).reshape(4, 64, 128)
        for j in range(4):
            s = 4 * blk + (j + row // 8) % 4
            own = jnp.logical_and(is_self, s == me16)

            @pl.when(own)
            def _():
                ret_local.start()

            @pl.when(jnp.logical_not(own))
            def _():
                ret_copy(s).start()

        return carry

    lax.fori_loop(0, 4, attend, 0)

    own_wo.wait()
    sib_page = page - core + 1 - core
    rcopy(wo_ref, wo_pad.at[sib_page, 32:112, :], loc_sem.at[1], loc_sem.at[2], sib).wait_recv()
    for dist in (1, 2, 3, 4):
        for direction in (0, 1):
            for half in (0, 1):
                if dist > z_limit(direction, half):
                    continue
                src_z = (zi - dist + 8) % 8 if direction == 0 else (zi + dist) % 8
                place = wo_pad.at[src_z * 2 + 1 - core, 32:112, half * 640 : half * 640 + 640]
                rcopy(
                    place, place, zf_send.at[direction, half, dist - 1],
                    zf_recv.at[direction, half, dist - 1], sib,
                ).wait_recv()

    def ret_take(h, carry):
        own = jnp.logical_and(is_self, h == me16)

        @pl.when(own)
        def _():
            ret_local.wait()

        @pl.when(jnp.logical_not(own))
        def _():
            rcopy(abuf.at[h], abuf.at[h], ret_send.at[h], ret_recv.at[h], sib).wait_recv()

        return carry

    lax.fori_loop(0, 16, ret_take, 0)
    attn = jnp.concatenate([abuf[h] for h in range(HEADS)], axis=1)
    hidden = res_ref[0].astype(F32) + jnp.dot(
        attn, wo_pad[...].reshape(HEADS * 128, D), preferred_element_type=F32
    )
    mean_sq = jnp.mean(hidden * hidden, axis=1, keepdims=True)
    normed = (hidden * lax.rsqrt(mean_sq + 1e-06) * gain_ref[...]).astype(BF16)
    dst_r = lax.broadcasted_iota(jnp.int32, (64, 64), 0)
    src_r = lax.broadcasted_iota(jnp.int32, (64, 64), 1)
    want = jnp.where(dst_r < 32, 2 * dst_r, 2 * dst_r - 63)
    select = jnp.where(src_r == want, 1.0, 0.0).astype(BF16)
    split = jnp.dot(select, normed, preferred_element_type=F32).astype(BF16)
    for xd in range(4):
        dj, fh = xd // 2, xd % 2
        nsend[xd] = split[32 * dj : 32 * dj + 32, 640 * fh : 640 * fh + 640]

    def xa_copy(j):
        return rcopy(
            nsend.at[(xi + j) % 4], nall.at[xi, yi], xa_send.at[j - 1], xa_recv.at[j - 1], xdev(j)
        )

    for j in (1, 3, 2):
        xa_copy(j).start()
    xa_local = pltpu.make_async_copy(nsend.at[xi], nall.at[xi, yi], loc_sem.at[3])
    xa_local.start()

    def y_slot(j, dist, direction):
        xs = (xi + 4 - j) % 4
        ys = (yi - dist + 8) % 8 if direction == 0 else (yi + dist) % 8
        return nall.at[xs, ys]

    def y_limit(j, direction):
        return 4 if direction == j // 2 else 3

    def y_copy(j, dist, direction):
        place = y_slot(j, dist - 1, direction)
        return rcopy(
            place, place, y_send.at[j, direction, dist - 1], y_recv.at[j, direction, dist - 1],
            y_right if direction == 0 else y_left,
        )

    def y_wait(j, dist, direction):
        place = y_slot(j, dist, direction)
        rcopy(
            place, place, y_send.at[j, direction, dist - 1], y_recv.at[j, direction, dist - 1], sib
        ).wait_recv()

    xa_local.wait()
    for j in (0, 1, 3, 2):
        if j:
            xs = (xi + 4 - j) % 4
            rcopy(
                nall.at[xs, yi], nall.at[xs, yi], xa_send.at[j - 1], xa_recv.at[j - 1], sib
            ).wait_recv()
        for direction in (0, 1):
            y_copy(j, 1, direction).start()
    for dist in (1, 2, 3, 4):
        for j in (0, 1, 3, 2):
            for direction in (0, 1):
                if dist > y_limit(j, direction):
                    continue
                y_wait(j, dist, direction)
                if dist < y_limit(j, direction):
                    y_copy(j, dist + 1, direction).start()
        if dist == 1:
            for j in (1, 3, 2):
                for di in (0, 1):
                    xs = (xi + 4 - j) % 4
                    lines = pl.ds(pl.multiple_of(core * 80, 16), 80)
                    place = wsl.at[xs, di, lines, :]
                    rcopy(
                        place, place, w_send.at[j - 1, di], w_recv.at[j - 1, di], sib
                    ).wait_recv()
                    w_fwd(j, di).start()
    for j in (1, 3, 2):
        for di in (0, 1):
            xs = (xi + 4 - j) % 4
            lines = pl.ds(pl.multiple_of((1 - core) * 80, 16), 80)
            place = wsl.at[xs, di, lines, :]
            rcopy(place, place, wf_send.at[j - 1, di], wf_recv.at[j - 1, di], sib).wait_recv()
    for di in (0, 1):
        w_local[di].wait()

    half_c = cols_n // 2
    half_f = half_c.astype(F32)

    def rs_copy(b, j):
        return rcopy(
            part_send.at[b, (xi + j) % 4], part_recv.at[b, j - 1],
            rs_send.at[b, j - 1], rs_recv.at[b, j - 1], xdev(j),
        )

    for b in (0, 1):
        first = 384 * b
        group = (256 * b + lax.broadcasted_iota(jnp.int32, (256, 640), 0)).astype(F32)
        place = (first + lax.broadcasted_iota(jnp.int32, (256, 640), 1)).astype(F32)
        band = jnp.floor((group + 0.5) / half_f)
        total = None
        window = nall[...].reshape(1024, 640)[first : first + 640]
        for di in (0, 1):
            want = band * half_f + group + di * half_f
            pick = jnp.where(place == want, 1.0, 0.0).astype(BF16)
            rows_g = jnp.dot(pick, window, preferred_element_type=F32).astype(BF16)
            term = nt(wsl[:, di].reshape(640, 640), rows_g)
            total = term if total is None else total + term
        pieces = total.reshape(4, 160, 256)
        own_part[b] = pieces
        part_send[b] = pieces.astype(BF16)
        for j in (1, 3, 2):
            rs_copy(b, j).start()

    eye = lax.broadcasted_iota(jnp.int32, (160, 160), 0) == lax.broadcasted_iota(
        jnp.int32, (160, 160), 1
    )
    bias = jnp.sum(jnp.where(eye, bias_ref[...], 0.0), axis=1, keepdims=True)
    live_groups = (rows_n // 2) * half_c
    for b in (0, 1):
        total = own_part[b, xi] + bias
        for j in (1, 3, 2):
            rcopy(
                part_send.at[b, 0], part_recv.at[b, j - 1],
                rs_send.at[b, j - 1], rs_recv.at[b, j - 1], sib,
            ).wait_recv()
            total = total + part_recv[b, j - 1].astype(F32)
        act = 0.5 * total * (1.0 + lax.erf(total * math.sqrt(0.5)))
        group = 256 * b + lax.broadcasted_iota(jnp.int32, (160, 256), 1)
        act = jnp.where(group < live_groups, act, 0.0)
        out_ref[0, :, 256 * b : 256 * b + 256] = act.astype(BF16)

    @pl.when(jnp.logical_not(is_self))
    def _():
        p1_copy(0).wait_send()

    def p1_sent(i, carry):
        p1_copy(i).wait_send()
        return carry

    lax.fori_loop(1, 16, p1_sent, 0)

    def sent(s, carry):
        fw_copy(s).wait_send()
        own = jnp.logical_and(is_self, s == me16)

        @pl.when(jnp.logical_not(own))
        def _():
            ret_copy(s).wait_send()

        return carry

    lax.fori_loop(0, 16, sent, 0)
    sib_wo.wait_send()
    for dist in (1, 2, 3, 4):
        for direction in (0, 1):
            for half in (0, 1):
                if dist <= z_limit(direction, half):
                    z_copy(dist, direction, half).wait_send()
                    z_fwd(dist, direction, half).wait_send()
            for j in range(4):
                if dist <= y_limit(j, direction):
                    y_copy(j, dist, direction).wait_send()
    for j in (1, 2, 3):
        xa_copy(j).wait_send()
        for di in (0, 1):
            w_copy(j, di).wait_send()
            w_fwd(j, di).wait_send()
            rs_copy(di, j).wait_send()


def local(qkv_rows, residual, out_weight, norm_gain, merge_weight, merge_bias, page_grid):
    vmem = pl.BlockSpec(memory_space=pltpu.VMEM)
    dma = pltpu.SemaphoreType.DMA
    return pl.pallas_call(
        kernel,
        out_shape=jax.ShapeDtypeStruct((1, 160, 512), BF16),
        in_specs=[pl.BlockSpec(memory_space=pltpu.SMEM)] + [vmem] * 5
        + [pl.BlockSpec(memory_space=pl.ANY)],
        out_specs=vmem,
        scratch_shapes=[
            pltpu.VMEM((16, 64, 256), BF16),
            pltpu.VMEM((2, 16, 64, 256), BF16),
            pltpu.VMEM((16, 64, 128), BF16),
            pltpu.VMEM((16, 64, 128), BF16),
            pltpu.VMEM((16, 128, D), BF16),
            pltpu.VMEM((4, 2, 160, 640), BF16),
            pltpu.VMEM((4, 32, 640), BF16),
            pltpu.VMEM((4, 8, 32, 640), BF16),
            pltpu.VMEM((2, 4, 160, 256), F32),
            pltpu.VMEM((2, 4, 160, 256), BF16),
            pltpu.VMEM((2, 3, 160, 256), BF16),
            dma((16,)), dma((16,)), dma((16,)), dma((16,)), dma((16,)), dma((16,)),
            dma((3, 2)), dma((3, 2)), dma((3, 2)), dma((3, 2)),
            dma((2, 2, 4)), dma((2, 2, 4)), dma((2, 2, 4)), dma((2, 2, 4)),
            dma((3,)), dma((3,)), dma((4, 2, 4)), dma((4, 2, 4)), dma((2, 3)), dma((2, 3)),
            dma((6,)),
        ],
        compiler_params=pltpu.CompilerParams(
            collective_id=0, has_side_effects=True, vmem_limit_bytes=48 * 1024 * 1024
        ),
        cost_estimate=pl.CostEstimate(
            flops=4 * 10**9, bytes_accessed=4 * 10**6, transcendentals=2 * 10**6
        ),
        name="sublayer",
    )(
        page_grid, qkv_rows, residual, out_weight, norm_gain.reshape(1, D),
        merge_bias.reshape(1, 160), merge_weight,
    )


def solution(mesh):
    in_specs = (
        P("page", "row", None),
        P("page", "row", None),
        P("page", None),
        P(),
        P("row", None),
        P("row"),
        P("page", None),
    )
    out_specs = P("page", "row", None)
    return jax.shard_map(local, mesh=mesh, in_specs=in_specs, out_specs=out_specs, check_vma=False)
```

time: 221 us -> 89.7 us (0.41)
  the two profiles are of different devices: /device:TPU:8 before, /device:TPU:4 now
where the time goes in v1:
time: 89.7 us; the launch traced here: 89.4 us
  Pallas kernels  82.4 us (92%)
  local copies, waits for them, and re-layouts  7.01 us (8%)
    pallas_call x1, Pallas kernels, local(): pl.pallas_call(kernel, out_shape=jax.ShapeDtypeStruct((1, 160, 512), BF16...  82.4 us
    unnamed x13, local copies, waits for them, and re-layouts  6.31 us

profile of v1, /device:TPU:4, one launch (start us, length us, event | category | flops | bytes accessed | tf_op | source)
XLA Modules:
  0.0 89.4 jit_solution(4703647319195041718)
XLA Ops:
  0.0 0.7 reshape.6.gain_ref
  0.7 0.0 copy-start
  0.7 1.4 %copy-done = bf16[160,5120]{1,0:T(8,128)(2,1)S(1)} copy-done((bf16[160,5120]{1,0:T(8,128)(2,1)S(1)}, bf16[160,5120]{1,0:T(8,128)(2,1)}, u32[]{:S(2)}) %copy-start) | copy-done | bytes 1638424
  2.1 0.0 copy-start.1
  2.1 1.0 %copy-done.1 = bf16[1,64,3840]{2,1,0:T(8,128)(2,1)S(1)} copy-done((bf16[1,64,3840]{2,1,0:T(8,128)(2,1)S(1)}, bf16[1,64,3840]{2,1,0:T(8,128)(2,1)}, u32[]{:S(2)}) %copy-start.1) | copy-done | bytes 491544
  3.2 0.0 copy-start.2
  3.2 0.9 %copy-done.2 = bf16[80,1280]{1,0:T(8,128)(2,1)S(1)} copy-done((bf16[80,1280]{1,0:T(8,128)(2,1)S(1)}, bf16[80,1280]{1,0:T(8,128)(2,1)}, u32[]{:S(2)}) %copy-start.2) | copy-done | bytes 204824
  4.1 0.0 copy-start.3
  4.1 0.9 %copy-done.3 = bf16[1,64,1280]{2,1,0:T(8,128)(2,1)S(1)} copy-done((bf16[1,64,1280]{2,1,0:T(8,128)(2,1)S(1)}, bf16[1,64,1280]{2,1,0:T(8,128)(2,1)}, u32[]{:S(2)}) %copy-start.3) | copy-done | bytes 163864
  5.0 0.0 copy-start.4
  5.0 0.7 copy-done.4
  5.7 0.0 copy-start.5
  5.7 0.7 copy-done.5
  6.3 82.4 %sublayer.1 = bf16[1,160,512]{2,1,0:T(8,128)(2,1)S(1)} custom-call(s32[1,2]{1,0:T(1,128)S(1)} %copy-done.5, bf16[1,64,3840]{2,1,0:T(8,128)(2,1)S(1)} %copy-done.1, bf16[1,64,1280]{2,1,0:T(8,128)(2,1)S(1)} %copy-done.3, bf16[80,1280]{1,0:T(8,128)(2,1)S(1)} %copy-done.2, f32[1,1280]{1,0:T(1,128)S(1)} %reshape.6.gain_ref, f32[1,160]{1,0:T(1,128)S(1)} %bitcast.1, ...), custom_call_target="tpu_custom_call" | custom-call | flops 4000000000 | bytes 4000000 | tf_op jit(solution)/shard_map/sublayer/pallas_call | solution.py:471
  88.7 0.7 copy.9
Async XLA Ops:
  0.7 1.4 %copy-start = (bf16[160,5120]{1,0:T(8,128)(2,1)S(1)}, bf16[160,5120]{1,0:T(8,128)(2,1)}, u32[]{:S(2)}) copy-start(bf16[160,5120]{1,0:T(8,128)(2,1)} %w_ref.1) | copy-start | bytes 4915204
  2.1 1.0 %copy-start.1 = (bf16[1,64,3840]{2,1,0:T(8,128)(2,1)S(1)}, bf16[1,64,3840]{2,1,0:T(8,128)(2,1)}, u32[]{:S(2)}) copy-start(bf16[1,64,3840]{2,1,0:T(8,128)(2,1)} %qkv_ref.1) | copy-start | bytes 1474564
  3.2 0.9 %copy-start.2 = (bf16[80,1280]{1,0:T(8,128)(2,1)S(1)}, bf16[80,1280]{1,0:T(8,128)(2,1)}, u32[]{:S(2)}) copy-start(bf16[80,1280]{1,0:T(8,128)(2,1)} %wo_ref.1) | copy-start | bytes 614404
  4.1 0.9 %copy-start.3 = (bf16[1,64,1280]{2,1,0:T(8,128)(2,1)S(1)}, bf16[1,64,1280]{2,1,0:T(8,128)(2,1)}, u32[]{:S(2)}) copy-start(bf16[1,64,1280]{2,1,0:T(8,128)(2,1)} %res_ref.1) | copy-start | bytes 491524
  5.0 0.7 copy-start.4
  5.7 0.7 copy-start.5

commit v2 on v1

v2 whole, which is shorter than its diff:
```python
import functools
import math

import jax
import jax.numpy as jnp
from jax import lax
from jax.experimental import pallas as pl
from jax.experimental.pallas import tpu as pltpu
from jax.sharding import PartitionSpec as P

D = 1280
HEADS = 16
HDIM = 80
MESH = pl.DeviceIdType.MESH
F32 = jnp.float32
BF16 = jnp.bfloat16
BIG = -1e30
ZORDER = (1, 7, 2, 6, 3, 5, 4)
ORDER = tuple((n // 4, n % 4) for n in range(1, 16)) + ((0, 0),)


def rcopy(src, dst, send_sem, recv_sem, dev):
    return pltpu.make_async_remote_copy(
        src_ref=src, dst_ref=dst, send_sem=send_sem, recv_sem=recv_sem,
        device_id=dev, device_id_type=MESH,
    )


def nt(a, b):
    return lax.dot_general(a, b, (((1,), (1,)), ((), ())), preferred_element_type=F32)


def kernel(
    grid_hbm, qkv_hbm, res_hbm, wo_ref, gain_hbm, bias_hbm, w_ref,
    out_ref,
    grid_ref, qkv_ref, res_ref, gain_ref, bias_ref,
    pack_buf, xbuf, qbuf, sbuf, obuf, abuf, wo_pad, wsl, nsend, nall, own_part, part_send, part_recv,
    p1_send, p1_recv, fw_send, fw_recv, ret_send, ret_recv,
    w_send, w_recv, wf_send, wf_recv,
    z_send, z_recv, zx_send, zx_recv, zf_send, zf_recv,
    xa_send, xa_recv, y_send, y_recv, rs_send, rs_recv, loc_sem,
):
    page = lax.axis_index("page")
    row = lax.axis_index("row")
    core = page % 2
    zi = page // 2
    par = row % 2
    me16 = row // 2
    xi = row // 8
    yi = row % 8
    peer_page = page - core + par
    sib = (page - core + 1 - core, row)
    is_self = par == core
    y_right = (page, xi * 8 + (yi + 1) % 8)
    y_left = (page, xi * 8 + (yi + 7) % 8)

    def zdev(dz):
        return ((zi + dz) % 8 * 2 + core, row)

    def xdev(j):
        return (page, ((xi + j) % 4) * 8 + yi)

    def peer(s):
        return (peer_page, 2 * s + core)

    pulls = [
        pltpu.make_async_copy(src, dst, loc_sem.at[7 + n])
        for n, (src, dst) in enumerate(
            (
                (grid_hbm, grid_ref), (qkv_hbm, qkv_ref), (res_hbm, res_ref),
                (gain_hbm, gain_ref), (bias_hbm, bias_ref),
            )
        )
    ]
    for pull in pulls:
        pull.start()

    own_wo = pltpu.make_async_copy(wo_ref, wo_pad.at[page, 32:112, :], loc_sem.at[0])
    own_wo.start()

    barrier = pltpu.get_barrier_semaphore()

    def greet(dev):
        pl.semaphore_signal(barrier, inc=1, device_id=dev, device_id_type=MESH)

    def next_y(j, direction):
        return (page, (xi + j) % 4 * 8 + (yi + 1 + 6 * direction) % 8)

    greet(sib)
    for dz in ZORDER:
        greet(zdev(dz))
    for j in range(4):
        greet(next_y(j, 0))
        greet(next_y(j, 1))

    def greet_peer(i, carry):
        greet(peer((me16 + i) % 16))
        return carry

    lax.fori_loop(1, 16, greet_peer, 0)

    @pl.when(jnp.logical_not(is_self))
    def _():
        greet(peer(me16))
        for j in (1, 2, 3):
            greet(xdev(j))

    pulls[0].wait()
    rows_n = grid_ref[0, 0]
    cols_n = grid_ref[0, 1]
    valid_len = rows_n * cols_n
    lane = lax.broadcasted_iota(jnp.int32, (64, 256), 1)
    slot = row * 64 + lax.broadcasted_iota(jnp.int32, (64, 256), 0)
    tail = jnp.where(
        lane == 240, jnp.where(slot < valid_len, 0.0, BIG), jnp.where(lane == 241, 1.0, 0.0)
    )

    def pack(h):
        val = tail
        for third in (2, 1, 0):
            start = third * D + h * HDIM
            base = pl.multiple_of(jnp.minimum(start // 128 * 128, 3 * D - 256), 128)
            dest = third * HDIM
            window = qkv_ref[0, :, pl.ds(base, 256)].astype(F32)
            window = pltpu.roll(window, (dest + 256 - (start - base)) % 256, axis=1)
            val = jnp.where((lane >= dest) & (lane < dest + HDIM), window, val)
        pack_buf[h] = val.astype(BF16)

    @pl.when(is_self)
    def _():
        pl.semaphore_wait(barrier, 31)

    @pl.when(jnp.logical_not(is_self))
    def _():
        pl.semaphore_wait(barrier, 35)

    my_col = pl.multiple_of(xi % 2 * 640, 128)
    other_col = pl.multiple_of(640 - xi % 2 * 640, 128)
    x_side = (page, (xi + 5 - 2 * core) % 4 * 8 + yi)

    def z_page(dz, of_core):
        return (zi + 8 - dz) % 8 * 2 + of_core

    def z_copy(dz):
        return rcopy(
            wo_pad.at[page, 32:112, pl.ds(my_col, 640)], wo_pad.at[page, 32:112, pl.ds(my_col, 640)],
            z_send.at[dz - 1], z_recv.at[dz - 1], zdev(dz),
        )

    def zx_copy(dz):
        place = wo_pad.at[z_page(dz, core), 32:112, pl.ds(my_col, 640)]
        return rcopy(place, place, zx_send.at[dz - 1], zx_recv.at[dz - 1], x_side)

    def zf_copy(dz, of_core):
        place = wo_pad.at[z_page(dz, of_core), 32:112, :]
        return rcopy(place, place, zf_send.at[dz - 1], zf_recv.at[dz - 1], sib)

    def z_step(dz):
        place = wo_pad.at[z_page(dz, core), 32:112, pl.ds(my_col, 640)]
        rcopy(place, place, z_send.at[dz - 1], z_recv.at[dz - 1], sib).wait_recv()
        zx_copy(dz).start()

    def zx_step(dz):
        place = wo_pad.at[z_page(dz, core), 32:112, pl.ds(other_col, 640)]
        rcopy(place, place, zx_send.at[dz - 1], zx_recv.at[dz - 1], sib).wait_recv()
        zf_copy(dz, core).start()

    half_y = yi // 2

    def p1_copy(n):
        dx, dy = ORDER[n]
        h = (xi + dx) % 4 * 4 + (half_y + dy) % 4
        return rcopy(
            pack_buf.at[h], xbuf.at[0, me16], p1_send.at[h], p1_recv.at[me16], peer(h)
        )

    p1_local = pltpu.make_async_copy(pack_buf.at[me16], xbuf.at[0, me16], p1_recv.at[me16])

    pulls[1].wait()
    for n in range(15):
        dx, dy = ORDER[n]
        pack((xi + dx) % 4 * 4 + (half_y + dy) % 4)
        p1_copy(n).start()
    pack(me16)

    @pl.when(is_self)
    def _():
        p1_local.start()

    @pl.when(jnp.logical_not(is_self))
    def _():
        p1_copy(15).start()

    own_wo.wait()
    for dz in ZORDER:
        z_copy(dz).start()

    def w_copy(j, di):
        xd = (xi + j) % 4
        col = pl.multiple_of((2 * di + xd // 2) * D + (xd % 2) * 640, 128)
        lines = pl.ds(pl.multiple_of(core * 80, 16), 80)
        return rcopy(
            w_ref.at[lines, pl.ds(col, 640)], wsl.at[xi, di, lines, :],
            w_send.at[j - 1, di], w_recv.at[j - 1, di], xdev(j),
        )

    def w_fwd(j, di):
        xs = (xi + 4 - j) % 4
        lines = pl.ds(pl.multiple_of(core * 80, 16), 80)
        place = wsl.at[xs, di, lines, :]
        return rcopy(place, place, wf_send.at[j - 1, di], wf_recv.at[j - 1, di], sib)

    for j in (1, 3, 2):
        for di in (0, 1):
            w_copy(j, di).start()
    w_local = []
    for di in (0, 1):
        col = pl.multiple_of((2 * di + xi // 2) * D + (xi % 2) * 640, 128)
        w_local.append(
            pltpu.make_async_copy(w_ref.at[:, pl.ds(col, 640)], wsl.at[xi, di], loc_sem.at[4 + di])
        )
        w_local[di].start()
    sib_wo = rcopy(wo_pad.at[page, 32:112, :], wo_pad.at[page, 32:112, :], loc_sem.at[1], loc_sem.at[2], sib)
    sib_wo.start()
    for h in range(HEADS):
        wo_pad[h, 0:32, :] = jnp.zeros((32, D), BF16)
        wo_pad[h, 112:128, :] = jnp.zeros((16, D), BF16)

    def fw_copy(s):
        return rcopy(xbuf.at[0, s], xbuf.at[1, s], fw_send.at[s], fw_recv.at[s], sib)

    def p1_take(n):
        dx, dy = ORDER[n]
        s = (xi + 4 - dx) % 4 * 4 + (half_y + 4 - dy) % 4
        rcopy(xbuf.at[0, s], xbuf.at[0, s], p1_send.at[s], p1_recv.at[s], sib).wait_recv()
        fw_copy(s).start()

    @pl.when(is_self)
    def _():
        p1_local.wait()
        fw_copy(me16).start()

    for n in range(15):
        p1_take(n)

    @pl.when(jnp.logical_not(is_self))
    def _():
        p1_take(15)

    for dz in ZORDER:
        z_step(dz)

    factor = math.log2(math.e) / math.sqrt(HDIM)
    lane_q = lax.broadcasted_iota(jnp.int32, (256, 256), 1)

    def owner(n):
        dx, dy = ORDER[n]
        return (xi + dx) % 4 * 4 + (half_y + dy) % 4

    def ret_copy(half, n):
        return rcopy(
            obuf.at[half, n], abuf.at[half, me16],
            ret_send.at[half, n], ret_recv.at[half, me16], peer(owner(n)),
        )

    def ret_local(half):
        return pltpu.make_async_copy(
            obuf.at[half, 15], abuf.at[half, me16], ret_recv.at[half, me16]
        )

    def rolled_queries(blk):
        half, first = blk // 2, blk % 2 * 8
        queries = jnp.concatenate(
            [xbuf[0, owner(n), 32 * half : 32 * half + 32] for n in range(first, first + 8)], axis=0
        )
        rolled = pltpu.roll(queries.astype(F32), HDIM, axis=1)
        return jnp.where(
            (lane_q >= HDIM) & (lane_q < 2 * HDIM), rolled, jnp.where(lane_q == 240, 1.0, 0.0)
        ).astype(BF16)

    for blk in range(4):
        qbuf[blk] = rolled_queries(blk)
        sbuf[blk] = nt(qbuf[blk], xbuf[0].reshape(1024, 256))

    def fw_take(s, carry):
        rcopy(xbuf.at[1, s], xbuf.at[1, s], fw_send.at[s], fw_recv.at[s], sib).wait_recv()
        return carry

    lax.fori_loop(0, 16, fw_take, 0)
    later = nt(qbuf[0], xbuf[1].reshape(1024, 256))
    for blk in range(4):
        there = later
        if blk < 3:
            later = nt(qbuf[blk + 1], xbuf[1].reshape(1024, 256))
        here = sbuf[blk]
        peak = jnp.maximum(
            jnp.max(here, axis=1, keepdims=True), jnp.max(there, axis=1, keepdims=True)
        )
        mixed = jnp.dot(
            jnp.exp2((here - peak) * factor).astype(BF16), xbuf[0].reshape(1024, 256),
            preferred_element_type=F32,
        ) + jnp.dot(
            jnp.exp2((there - peak) * factor).astype(BF16), xbuf[1].reshape(1024, 256),
            preferred_element_type=F32,
        )
        mixed = mixed[:, 128:]
        mixed = mixed / mixed[:, 113:114]
        half, first = blk // 2, blk % 2 * 8
        obuf[half, first : first + 8] = mixed.astype(BF16).reshape(8, 32, 128)
        for n in range(first, min(first + 8, 15)):
            ret_copy(half, n).start()

    @pl.when(is_self)
    def _():
        ret_local(0).start()
        ret_local(1).start()

    @pl.when(jnp.logical_not(is_self))
    def _():
        ret_copy(0, 15).start()
        ret_copy(1, 15).start()

    for dz in ZORDER:
        zx_step(dz)

    for j in (1, 3, 2):
        for di in (0, 1):
            xs = (xi + 4 - j) % 4
            lines = pl.ds(pl.multiple_of(core * 80, 16), 80)
            place = wsl.at[xs, di, lines, :]
            rcopy(place, place, w_send.at[j - 1, di], w_recv.at[j - 1, di], sib).wait_recv()
            w_fwd(j, di).start()

    sib_page = page - core + 1 - core
    rcopy(wo_ref, wo_pad.at[sib_page, 32:112, :], loc_sem.at[1], loc_sem.at[2], sib).wait_recv()
    for dz in ZORDER:
        zf_copy(dz, 1 - core).wait_recv()
    pulls[2].wait()
    pulls[3].wait()
    dst_r = lax.broadcasted_iota(jnp.int32, (32, 32), 0)
    src_r = lax.broadcasted_iota(jnp.int32, (32, 32), 1)
    want = jnp.where(dst_r < 16, 2 * dst_r, 2 * dst_r - 31)
    select = jnp.where(src_r == want, 1.0, 0.0).astype(BF16)

    def project(half):
        def ret_take(h, carry):
            own = jnp.logical_and(is_self, h == me16)

            @pl.when(own)
            def _():
                ret_local(half).wait()

            @pl.when(jnp.logical_not(own))
            def _():
                rcopy(
                    abuf.at[half, h], abuf.at[half, h],
                    ret_send.at[half, h], ret_recv.at[half, h], sib,
                ).wait_recv()

            return carry

        lax.fori_loop(0, 16, ret_take, 0)
        attn = jnp.concatenate([abuf[half, h] for h in range(HEADS)], axis=1)
        hidden = res_ref[0, 32 * half : 32 * half + 32].astype(F32) + jnp.dot(
            attn, wo_pad[...].reshape(HEADS * 128, D), preferred_element_type=F32
        )
        mean_sq = jnp.mean(hidden * hidden, axis=1, keepdims=True)
        normed = (hidden * lax.rsqrt(mean_sq + 1e-06) * gain_ref[...].reshape(1, D)).astype(BF16)
        split = jnp.dot(select, normed, preferred_element_type=F32).astype(BF16)
        for xd in range(4):
            dj, fh = xd // 2, xd % 2
            nsend[half, xd] = split[16 * dj : 16 * dj + 16, 640 * fh : 640 * fh + 640]

    def xa_copy(half, j):
        return rcopy(
            nsend.at[half, (xi + j) % 4], nall.at[xi, yi, 16 * half : 16 * half + 16],
            xa_send.at[half, j - 1], xa_recv.at[half, j - 1], xdev(j),
        )

    def xa_local(half):
        return pltpu.make_async_copy(
            nsend.at[half, xi], nall.at[xi, yi, 16 * half : 16 * half + 16], loc_sem.at[3 * half + 3]
        )

    def y_slot(half, j, dist, direction):
        xs = (xi + 4 - j) % 4
        ys = (yi - dist + 8) % 8 if direction == 0 else (yi + dist) % 8
        return nall.at[xs, ys, 16 * half : 16 * half + 16]

    def y_limit(j, direction):
        return 4 if direction == j // 2 else 3

    def y_copy(half, j, dist, direction):
        if dist == 1:
            return rcopy(
                nsend.at[half, (xi + j) % 4], nall.at[xi, yi, 16 * half : 16 * half + 16],
                y_send.at[half, j, direction, 0], y_recv.at[half, j, direction, 0],
                next_y(j, direction),
            )
        place = y_slot(half, j, dist - 1, direction)
        return rcopy(
            place, place, y_send.at[half, j, direction, dist - 1],
            y_recv.at[half, j, direction, dist - 1], y_right if direction == 0 else y_left,
        )

    def y_wait(half, j, dist, direction):
        place = y_slot(half, j, dist, direction)
        rcopy(
            place, place, y_send.at[half, j, direction, dist - 1],
            y_recv.at[half, j, direction, dist - 1], sib,
        ).wait_recv()

    for half in (0, 1):
        project(half)
        for j in (0, 1, 3, 2):
            for direction in (0, 1):
                y_copy(half, j, 1, direction).start()
        for j in (1, 3, 2):
            xa_copy(half, j).start()
        xa_local(half).start()

    for dist in (1, 2, 3, 4):
        for half in (0, 1):
            for j in (0, 1, 3, 2):
                for direction in (0, 1):
                    if dist > y_limit(j, direction):
                        continue
                    y_wait(half, j, dist, direction)
                    if dist < y_limit(j, direction):
                        y_copy(half, j, dist + 1, direction).start()
    for half in (0, 1):
        xa_local(half).wait()
        for j in (1, 2, 3):
            place = y_slot(half, j, 0, 0)
            rcopy(
                place, place, xa_send.at[half, j - 1], xa_recv.at[half, j - 1], sib
            ).wait_recv()
    for j in (1, 3, 2):
        for di in (0, 1):
            xs = (xi + 4 - j) % 4
            lines = pl.ds(pl.multiple_of((1 - core) * 80, 16), 80)
            place = wsl.at[xs, di, lines, :]
            rcopy(place, place, wf_send.at[j - 1, di], wf_recv.at[j - 1, di], sib).wait_recv()
    for di in (0, 1):
        w_local[di].wait()

    half_c = cols_n // 2
    half_f = half_c.astype(F32)

    def rs_copy(b, j):
        return rcopy(
            part_send.at[b, (xi + j) % 4], part_recv.at[b, j - 1],
            rs_send.at[b, j - 1], rs_recv.at[b, j - 1], xdev(j),
        )

    for b in range(4):
        first = (0, 128, 384, 512)[b]
        group = (128 * b + lax.broadcasted_iota(jnp.int32, (128, 512), 0)).astype(F32)
        place = (first + lax.broadcasted_iota(jnp.int32, (128, 512), 1)).astype(F32)
        band = jnp.floor((group + 0.5) / half_f)
        total = None
        window = nall[...].reshape(1024, 640)[first : first + 512]
        for di in (0, 1):
            want = band * half_f + group + di * half_f
            pick = jnp.where(place == want, 1.0, 0.0).astype(BF16)
            rows_g = jnp.dot(pick, window, preferred_element_type=F32).astype(BF16)
            term = nt(wsl[:, di].reshape(640, 640), rows_g)
            total = term if total is None else total + term
        pieces = total.reshape(4, 160, 128)
        own_part[b] = pieces
        part_send[b] = pieces.astype(BF16)
        for j in (1, 3, 2):
            rs_copy(b, j).start()

    eye = lax.broadcasted_iota(jnp.int32, (160, 160), 0) == lax.broadcasted_iota(
        jnp.int32, (160, 160), 1
    )
    pulls[4].wait()
    bias = jnp.sum(jnp.where(eye, bias_ref[...].reshape(1, 160), 0.0), axis=1, keepdims=True)
    live_groups = (rows_n // 2) * half_c
    for b in range(4):
        total = own_part[b, xi] + bias
        for j in (1, 3, 2):
            rcopy(
                part_send.at[b, 0], part_recv.at[b, j - 1],
                rs_send.at[b, j - 1], rs_recv.at[b, j - 1], sib,
            ).wait_recv()
            total = total + part_recv[b, j - 1].astype(F32)
        act = 0.5 * total * (1.0 + lax.erf(total * math.sqrt(0.5)))
        group = 128 * b + lax.broadcasted_iota(jnp.int32, (160, 128), 1)
        act = jnp.where(group < live_groups, act, 0.0)
        out_ref[0, :, 128 * b : 128 * b + 128] = act.astype(BF16)

    for n in range(15):
        p1_copy(n).wait_send()

    @pl.when(jnp.logical_not(is_self))
    def _():
        p1_copy(15).wait_send()

    def sent(s, carry):
        fw_copy(s).wait_send()
        return carry

    lax.fori_loop(0, 16, sent, 0)
    for half in (0, 1):
        for n in range(15):
            ret_copy(half, n).wait_send()

        @pl.when(jnp.logical_not(is_self))
        def _():
            ret_copy(half, 15).wait_send()

    sib_wo.wait_send()
    for dz in ZORDER:
        z_copy(dz).wait_send()
        zx_copy(dz).wait_send()
        zf_copy(dz, core).wait_send()
    for half in (0, 1):
        for j in range(4):
            for direction in (0, 1):
                for dist in range(1, y_limit(j, direction) + 1):
                    y_copy(half, j, dist, direction).wait_send()
    for j in (1, 2, 3):
        for di in (0, 1):
            xa_copy(di, j).wait_send()
            w_copy(j, di).wait_send()
            w_fwd(j, di).wait_send()
            rs_copy(di, j).wait_send()
            rs_copy(di + 2, j).wait_send()


def local(qkv_rows, residual, out_weight, norm_gain, merge_weight, merge_bias, page_grid):
    vmem = pl.BlockSpec(memory_space=pltpu.VMEM)
    dma = pltpu.SemaphoreType.DMA
    return pl.pallas_call(
        kernel,
        out_shape=jax.ShapeDtypeStruct((1, 160, 512), BF16),
        in_specs=[pl.BlockSpec(memory_space=pltpu.HBM)] * 7,
        out_specs=vmem,
        scratch_shapes=[
            pltpu.SMEM((1, 2), jnp.int32),
            pltpu.VMEM((1, 64, 3 * D), BF16),
            pltpu.VMEM((1, 64, D), BF16),
            pltpu.VMEM((D,), F32),
            pltpu.VMEM((160,), F32),
            pltpu.VMEM((16, 64, 256), BF16),
            pltpu.VMEM((2, 16, 64, 256), BF16),
            pltpu.VMEM((4, 256, 256), BF16),
            pltpu.VMEM((4, 256, 1024), F32),
            pltpu.VMEM((2, 16, 32, 128), BF16),
            pltpu.VMEM((2, 16, 32, 128), BF16),
            pltpu.VMEM((16, 128, D), BF16),
            pltpu.VMEM((4, 2, 160, 640), BF16),
            pltpu.VMEM((2, 4, 16, 640), BF16),
            pltpu.VMEM((4, 8, 32, 640), BF16),
            pltpu.VMEM((4, 4, 160, 128), F32),
            pltpu.VMEM((4, 4, 160, 128), BF16),
            pltpu.VMEM((4, 3, 160, 128), BF16),
            dma((16,)), dma((16,)), dma((16,)), dma((16,)), dma((2, 16)), dma((2, 16)),
            dma((3, 2)), dma((3, 2)), dma((3, 2)), dma((3, 2)),
            dma((7,)), dma((7,)), dma((7,)), dma((7,)), dma((7,)), dma((7,)),
            dma((2, 3)), dma((2, 3)), dma((2, 4, 2, 4)), dma((2, 4, 2, 4)), dma((4, 3)), dma((4, 3)),
            dma((12,)),
        ],
        compiler_params=pltpu.CompilerParams(
            collective_id=0, has_side_effects=True, vmem_limit_bytes=60 * 1024 * 1024
        ),
        cost_estimate=pl.CostEstimate(
            flops=4 * 10**9, bytes_accessed=4 * 10**6, transcendentals=2 * 10**6
        ),
        name="sublayer",
    )(
        page_grid, qkv_rows, residual, out_weight, norm_gain, merge_bias, merge_weight,
    )


def solution(mesh):
    in_specs = (
        P("page", "row", None),
        P("page", "row", None),
        P("page", None),
        P(),
        P("row", None),
        P("row"),
        P("page", None),
    )
    out_specs = P("page", "row", None)
    return jax.shard_map(local, mesh=mesh, in_specs=in_specs, out_specs=out_specs, check_vma=False)
```

time: 89.7 us -> 79.6 us (0.89)
  the two profiles are of different devices: /device:TPU:4 before, /device:TPU:16 now
where the time goes in v2:
time: 79.6 us; the launch traced here: 79.4 us
  Pallas kernels  77.8 us (98%)
  local copies, waits for them, and re-layouts  1.59 us (2%)
    pallas_call x1, Pallas kernels, local(): pl.pallas_call(kernel, out_shape=jax.ShapeDtypeStruct((1, 160, 512), BF16...  77.8 us
    unnamed x1, local copies, waits for them, and re-layouts  1.59 us

profile of v2, /device:TPU:16, one launch (start us, length us, event | category | flops | bytes accessed | tf_op | source)
XLA Modules:
  0.0 79.4 jit_solution(5591975637627639211)
XLA Ops:
  0.0 77.8 %sublayer.1 = bf16[1,160,512]{2,1,0:T(8,128)(2,1)} custom-call(s32[1,2]{1,0:T(1,128)} %grid_hbm.1, bf16[1,64,3840]{2,1,0:T(8,128)(2,1)} %qkv_hbm.1, bf16[1,64,1280]{2,1,0:T(8,128)(2,1)} %res_hbm.1, bf16[80,1280]{1,0:T(8,128)(2,1)} %wo_ref.1, f32[1280]{0:T(1024)} %gain_hbm.1, f32[160]{0:T(256)} %bias_hbm.1, bf16[160,5120]{1,0:T(8,128)(2,1)} %w_ref.1), custom_call_target="tpu_custom_call" | custom-call | flops 4000000000 | bytes 4000000 | tf_op jit(solution)/shard_map/sublayer/pallas_call | solution.py:536
  77.8 1.6 %copy.9 = bf16[1,160,512]{2,1,0:T(8,128)(2,1)} copy(bf16[1,160,512]{2,1,0:T(8,128)(2,1)} %sublayer.1) | data formatting | bytes 327680

commit v3 on v2

--- a/solution.py
+++ b/solution.py
@@ -176,6 +176,9 @@
 
     p1_local = pltpu.make_async_copy(pack_buf.at[me16], xbuf.at[0, me16], p1_recv.at[me16])
 
+    own_wo.wait()
+    for dz in ZORDER:
+        z_copy(dz).start()
     pulls[1].wait()
     for n in range(15):
         dx, dy = ORDER[n]
@@ -191,9 +194,6 @@
     def _():
         p1_copy(15).start()
 
-    own_wo.wait()
-    for dz in ZORDER:
-        z_copy(dz).start()
 
     def w_copy(j, di):
         xd = (xi + j) % 4
@@ -472,6 +472,42 @@
         for j in (1, 3, 2):
             rs_copy(b, j).start()
 
+    for n in range(15):
+        p1_copy(n).wait_send()
+
+    @pl.when(jnp.logical_not(is_self))
+    def _():
+        p1_copy(15).wait_send()
+
+    def sent(s, carry):
+        fw_copy(s).wait_send()
+        return carry
+
+    lax.fori_loop(0, 16, sent, 0)
+    for half in (0, 1):
+        for n in range(15):
+            ret_copy(half, n).wait_send()
+
+        @pl.when(jnp.logical_not(is_self))
+        def _():
+            ret_copy(half, 15).wait_send()
+
+    sib_wo.wait_send()
+    for dz in ZORDER:
+        z_copy(dz).wait_send()
+        zx_copy(dz).wait_send()
+        zf_copy(dz, core).wait_send()
+    for half in (0, 1):
+        for j in range(4):
+            for direction in (0, 1):
+                for dist in range(1, y_limit(j, direction) + 1):
+                    y_copy(half, j, dist, direction).wait_send()
+    for j in (1, 2, 3):
+        for di in (0, 1):
+            xa_copy(di, j).wait_send()
+            w_copy(j, di).wait_send()
+            w_fwd(j, di).wait_send()
+
     eye = lax.broadcasted_iota(jnp.int32, (160, 160), 0) == lax.broadcasted_iota(
         jnp.int32, (160, 160), 1
     )
@@ -491,43 +527,9 @@
         act = jnp.where(group < live_groups, act, 0.0)
         out_ref[0, :, 128 * b : 128 * b + 128] = act.astype(BF16)
 
-    for n in range(15):
-        p1_copy(n).wait_send()
-
-    @pl.when(jnp.logical_not(is_self))
-    def _():
-        p1_copy(15).wait_send()
-
-    def sent(s, carry):
-        fw_copy(s).wait_send()
-        return carry
-
-    lax.fori_loop(0, 16, sent, 0)
-    for half in (0, 1):
-        for n in range(15):
-            ret_copy(half, n).wait_send()
-
-        @pl.when(jnp.logical_not(is_self))
-        def _():
-            ret_copy(half, 15).wait_send()
-
-    sib_wo.wait_send()
-    for dz in ZORDER:
-        z_copy(dz).wait_send()
-        zx_copy(dz).wait_send()
-        zf_copy(dz, core).wait_send()
-    for half in (0, 1):
-        for j in range(4):
-            for direction in (0, 1):
-                for dist in range(1, y_limit(j, direction) + 1):
-                    y_copy(half, j, dist, direction).wait_send()
-    for j in (1, 2, 3):
-        for di in (0, 1):
-            xa_copy(di, j).wait_send()
-            w_copy(j, di).wait_send()
-            w_fwd(j, di).wait_send()
-            rs_copy(di, j).wait_send()
-            rs_copy(di + 2, j).wait_send()
+    for b in range(4):
+        for j in (1, 2, 3):
+            rs_copy(b, j).wait_send()
 
 
 def local(qkv_rows, residual, out_weight, norm_gain, merge_weight, merge_bias, page_grid):

time: 79.6 us -> 77.5 us (0.974)
  Pallas kernels: 77.8 us -> 75.7 us
    pallas_call x1, Pallas kernels: 77.8 us -> 75.7 us  [local(): pl.pallas_call(kernel, out_shape=jax.ShapeDtypeStruct((1, 160, 512), BF16...]
where the time goes in v3:
time: 77.5 us; the launch traced here: 77.3 us
  Pallas kernels  75.7 us (98%)
  local copies, waits for them, and re-layouts  1.59 us (2%)
    pallas_call x1, Pallas kernels, local(): pl.pallas_call(kernel, out_shape=jax.ShapeDtypeStruct((1, 160, 512), BF16...  75.7 us
    unnamed x1, local copies, waits for them, and re-layouts  1.59 us

profile of v3, /device:TPU:16, one launch (start us, length us, event | category | flops | bytes accessed | tf_op | source)
XLA Modules:
  0.0 77.3 jit_solution(3301733871715163217)
XLA Ops:
  0.0 75.7 %sublayer.1 = bf16[1,160,512]{2,1,0:T(8,128)(2,1)} custom-call(s32[1,2]{1,0:T(1,128)} %grid_hbm.1, bf16[1,64,3840]{2,1,0:T(8,128)(2,1)} %qkv_hbm.1, bf16[1,64,1280]{2,1,0:T(8,128)(2,1)} %res_hbm.1, bf16[80,1280]{1,0:T(8,128)(2,1)} %wo_ref.1, f32[1280]{0:T(1024)} %gain_hbm.1, f32[160]{0:T(256)} %bias_hbm.1, bf16[160,5120]{1,0:T(8,128)(2,1)} %w_ref.1), custom_call_target="tpu_custom_call" | custom-call | flops 4000000000 | bytes 4000000 | tf_op jit(solution)/shard_map/sublayer/pallas_call | solution.py:538
  75.7 1.6 %copy.9 = bf16[1,160,512]{2,1,0:T(8,128)(2,1)} copy(bf16[1,160,512]{2,1,0:T(8,128)(2,1)} %sublayer.1) | data formatting | bytes 327680
